TPU v7x, 32 devices: a whole 2x2x4 slice. The times are simulated.
32 devices in a mesh: narrow: 1, wide: 32 (over z, y, x, core).
Axes of the slice: x: 2, y: 2, z: 4, core: 2. Of those that a mesh axis runs over, the one named last changes fastest.
Arguments:
- pair_act: float32 [256, 256, 128], P('narrow', 'wide'), may hold values from -6 to 6
- block_mask: int32 [4, 4], replicated, may hold values from 0 to 1, as said below
- left_weight: bfloat16 [128, 256], replicated, may hold values from -0.5 to 0.5
- right_weight: bfloat16 [128, 256], replicated, may hold values from -0.5 to 0.5
- gate_weight: bfloat16 [128, 128], replicated, may hold values from -0.5 to 0.5
- out_weight: bfloat16 [128, 128], replicated, may hold values from -0.5 to 0.5
Outputs:
- update: float32 [256, 256, 128], P('narrow', 'wide')
Inputs may be any that keep to these rules, and one draw needn't show every extreme that they name: `block_mask`: 0 or 1, symmetric; tokens are grouped into up to 4 chains of whole blocks in order, the first chain covering more than half of the blocks; every diagonal block is 1, and all blocks of one pair of chains share a value.
All inputs are finite; a program needn't handle non-finite values.
Results may differ from a plain program's by a relative error of at most 0.008.
Values may be sent and summed in bfloat16 or wider, within the bound.
No kernel may reach another device: no remote copies, remote signals or barrier semaphores. Data moves between devices by JAX's collectives and lax.ppermute only.
A program may use at most 64 MiB of HBM per device.

v0:
```python
import jax
import jax.numpy as jnp
from jax import lax
from jax.sharding import PartitionSpec as P

C = 128
BLOCK = 64


def layer_norm(values):
    centre = jnp.mean(values, axis=-1, keepdims=True)
    spread = jnp.mean(jnp.square(values - centre), axis=-1, keepdims=True)
    return (values - centre) * jax.lax.rsqrt(spread + 1e-05)


def gated_projection(normed, weight, channels):
    mixed_proj = jnp.dot(normed, weight, preferred_element_type=jnp.float32)
    return jax.nn.sigmoid(mixed_proj[:, :channels]) * mixed_proj[:, channels:]


def on_device(pair_act, block_mask, left_weight, right_weight, gate_weight, out_weight):
    tile_rows = pair_act.shape[0]
    tile_cols = pair_act.shape[1]
    row_ids = lax.axis_index("narrow") * tile_rows + jnp.arange(tile_rows, dtype=jnp.int32)
    col_ids = lax.axis_index("wide") * tile_cols + jnp.arange(tile_cols, dtype=jnp.int32)
    block_ids = jnp.arange(block_mask.shape[0], dtype=jnp.int32)
    row_hot = (row_ids[:, None] // BLOCK == block_ids[None, :]).astype(jnp.float32)
    col_hot = (col_ids[:, None] // BLOCK == block_ids[None, :]).astype(jnp.float32)
    row_blocks = jnp.dot(row_hot, block_mask.astype(jnp.float32))
    tile_mask = jnp.dot(row_blocks, col_hot.T)
    normed = layer_norm(pair_act).astype(jnp.bfloat16).reshape(tile_rows * tile_cols, C)
    left_proj = (
        gated_projection(normed, left_weight, C).reshape(tile_rows, tile_cols, C)
        * tile_mask[:, :, None]
    ).astype(jnp.bfloat16)
    right_proj = (
        gated_projection(normed, right_weight, C).reshape(tile_rows, tile_cols, C)
        * tile_mask[:, :, None]
    ).astype(jnp.bfloat16)
    gate_act = jax.nn.sigmoid(jnp.dot(normed, gate_weight, preferred_element_type=jnp.float32))
    right_all = lax.all_gather(right_proj, "narrow", axis=0, tiled=True)
    right_cols = lax.all_to_all(right_all, "wide", split_axis=0, concat_axis=1, tiled=True)
    tri_sum = jnp.einsum(
        "ikc,jkc->ijc",
        lax.all_gather(left_proj, "wide", axis=1, tiled=True),
        right_cols,
        preferred_element_type=jnp.float32,
    )
    tri_normed = layer_norm(tri_sum).astype(jnp.bfloat16).reshape(tile_rows * tile_cols, C)
    update = gate_act * jnp.dot(tri_normed, out_weight, preferred_element_type=jnp.float32)
    return update.reshape(tile_rows, tile_cols, C)


def solution(mesh):
    return jax.shard_map(
        on_device,
        mesh=mesh,
        in_specs=(P("narrow", "wide", None), P(), P(), P(), P(), P()),
        out_specs=P("narrow", "wide", None),
        check_vma=False,
    )
```

profile of v0, /device:TPU:0, one launch (start us, length us, event | category | flops | bytes accessed | tf_op | source)
XLA Modules:
  0.0 179.0 jit_solution(3586450425503746546)
XLA Ops:
  6.5 1.7 reduce_sum.36
  8.3 0.1 copy.39
  8.4 0.6 multiply_reduce_fusion.1
  9.1 0.1 copy.41
  9.3 0.6 fusion.15
  9.9 0.4 fusion.23
  10.3 0.3 fusion.11
  10.6 0.6 copy.42
  11.2 0.4 fusion.24
  11.7 1.3 fusion.7
  12.9 1.7 copy.45
  14.7 0.3 fusion.4
  15.0 1.0 multiply_convert_fusion.1
  16.0 1.3 copy.43
  17.3 7.3 %all-to-all-start = ((bf16[256,8,128]{2,1,0:T(8,128)(2,1)}), bf16[256,8,128]{2,1,0:T(8,128)(2,1)S(1)}, u32[]{:S(2)}, u32[]{:S(2)}) async-start(bf16[256,8,128]{2,1,0:T(8,128)(2,1)} %copy.43), calls=%async_computation | async-start | bytes 1048576 | tf_op jit(solution)/shard_map/all_to_all | solution.py:42
  24.6 0.4 fusion.2
  25.1 20.2 %all-to-all-done = bf16[256,8,128]{2,1,0:T(8,128)(2,1)S(1)} async-done(((bf16[256,8,128]{2,1,0:T(8,128)(2,1)}), bf16[256,8,128]{2,1,0:T(8,128)(2,1)S(1)}, u32[]{:S(2)}, u32[]{:S(2)}) %all-to-all-start) | async-done | bytes 524320 | tf_op jit(solution)/shard_map/all_to_all | solution.py:42
  45.4 0.4 copy.46
  45.8 116.2 %all-gather.2.cloned.1.call-done = bf16[256,256,128]{0,1,2:T(8,128)(2,1)} async-done(((bf16[256,8,128]{0,1,2:T(8,128)(2,1)}), bf16[256,256,128]{0,1,2:T(8,128)(2,1)}) %all-gather.2.cloned.1.call-update) | async-done | bytes 16777232 | tf_op jit(solution)/shard_map/all_gather | solution.py:45
  162.0 8.0 %fusion.22 = (f32[256,8]{0,1:T(8,128)S(1)}, f32[256,8,128]{0,1,2:T(8,128)S(1)}) fusion(bf16[8,256,128]{1,0,2:T(8,128)(2,1)S(1)} %copy.46, bf16[256,256,128]{0,1,2:T(8,128)(2,1)} %all-gather.2.cloned.1.call-done), kind=kOutput, calls=%fused_computation.47 | convolution fusion | flops 134477824 | bytes 18358272 | tf_op jit(solution)/shard_map/ikc,jkc->ijc/dot_general | solution.py:43
  170.0 0.2 multiply_reduce_fusion
  170.2 0.1 multiply_convert_fusion
  170.3 0.6 copy.47
  170.9 1.3 fusion.3
  (23 shorter events, 0.3 us)
Async XLA Ops:
  6.5 3.4 %copy-start = (bf16[128,256]{1,0:T(8,128)(2,1)S(1)}, bf16[128,256]{1,0:T(8,128)(2,1)}, u32[]{:S(2)}) copy-start(bf16[128,256]{1,0:T(8,128)(2,1)} %param.9) | copy-start | bytes 196612
  6.5 1.9 %copy-start.1 = (f32[256,8,128]{2,1,0:T(8,128)S(1)}, f32[256,8,128]{2,1,0:T(8,128)}, u32[]{:S(2)}) copy-start(f32[256,8,128]{2,1,0:T(8,128)} %param.6) | copy-start | bytes 3145732
  6.5 155.4 %all-gather.2.cloned.1.call-start = ((), (), s32[]{:S(2)}) async-start(), calls=%async_computation.1 | async-start | bytes 17301504 | tf_op jit(solution)/shard_map/all_gather | solution.py:45
  10.3 0.9 copy-start.2
  11.6 3.0 %copy-start.5 = (s32[4,4]{1,0:T(4,128)S(1)}, s32[4,4]{1,0:T(4,128)}, u32[]{:S(2)}) copy-start(s32[4,4]{1,0:T(4,128)} %param.7) | copy-start | bytes 196
  16.0 8.7 %copy-start.4 = (bf16[128,128]{1,0:T(8,128)(2,1)S(1)}, bf16[128,128]{1,0:T(8,128)(2,1)}, u32[]{:S(2)}) copy-start(bf16[128,128]{1,0:T(8,128)(2,1)} %param.10) | copy-start | bytes 98308
  17.3 27.9 %all-to-all-start = ((bf16[256,8,128]{2,1,0:T(8,128)(2,1)}), bf16[256,8,128]{2,1,0:T(8,128)(2,1)S(1)}, u32[]{:S(2)}, u32[]{:S(2)}) async-start(bf16[256,8,128]{2,1,0:T(8,128)(2,1)} %copy.43), calls=%async_computation | async-start | bytes 1048576 | tf_op jit(solution)/shard_map/all_to_all | solution.py:42
  170.0 0.9 copy-start.3
Sparse Core Ops, SparseCore 0:
  16.1 145.7 all-gather.1
where the time goes:
time: 179 us
  waiting for transfers between devices  136 us (76%)
  between operations  13.6 us (8%)
  matrix products  10.9 us (6%)
  starting transfers between devices  7.3 us (4%)
  other arithmetic  5.72 us (3%)
  local copies, waits for them, and re-layouts  5.1 us (3%)
    all_gather x1, waiting for transfers between devices, on_device(): lax.all_gather(left_proj, 'wide', axis=1, tiled=True)  116 us
    all_to_all x1, waiting for transfers between devices, on_device(): lax.all_to_all(right_all, 'wide', split_axis=0, concat_axis=1, tiled=True)  20.2 us
    dot_general x1, matrix products, on_device(): jnp.einsum('ikc,jkc->ijc', lax.all_gather(left_proj, 'wide', axis=1, tile...  8.04 us
    all_to_all x1, starting transfers between devices, on_device(): lax.all_to_all(right_all, 'wide', split_axis=0, concat_axis=1, tiled=True)  7.3 us
  transfers between devices with their start and end apart: 2, of which 2 were waited for; matrix products, arithmetic and copies ran while one was open for 1% of the time, Pallas kernels for 0%

commit v1 on v0

v1 whole, which is shorter than its diff:
```python
import jax
import jax.numpy as jnp
from jax import lax
from jax.sharding import PartitionSpec as P

C = 128
BLOCK = 64


def on_device(pair_act, block_mask, left_weight, right_weight, gate_weight, out_weight):
    tile_rows = pair_act.shape[0]
    tile_cols = pair_act.shape[1]
    wide = lax.axis_size("wide")
    narrow = lax.axis_size("narrow")
    per_device = C // wide
    row_ids = lax.axis_index("narrow") * tile_rows + jnp.arange(tile_rows, dtype=jnp.int32)
    col_ids = lax.axis_index("wide") * tile_cols + jnp.arange(tile_cols, dtype=jnp.int32)
    block_ids = jnp.arange(block_mask.shape[0], dtype=jnp.int32)
    row_hot = (row_ids[:, None] // BLOCK == block_ids[None, :]).astype(jnp.float32)
    col_hot = (col_ids[:, None] // BLOCK == block_ids[None, :]).astype(jnp.float32)
    tile_mask = jnp.dot(jnp.dot(row_hot, block_mask.astype(jnp.float32)), col_hot.T).T

    centre = jnp.mean(pair_act, axis=-1, keepdims=True)
    spread = jnp.mean(jnp.square(pair_act - centre), axis=-1, keepdims=True)
    normed = ((pair_act - centre) * lax.rsqrt(spread + 1e-05)).astype(jnp.bfloat16)

    def edges(weight):
        mixed = jnp.einsum("cd,ikc->dki", weight, normed, preferred_element_type=jnp.float32)
        proj = jax.nn.sigmoid(mixed[:C]) * mixed[C:] * tile_mask[None]
        return proj.astype(jnp.bfloat16).reshape(wide, per_device, tile_cols, tile_rows)

    send = jnp.stack([edges(left_weight), edges(right_weight)], axis=1)
    recv = lax.all_to_all(send, "wide", split_axis=0, concat_axis=0, tiled=True)
    left, right = recv[:, 0], recv[:, 1]
    if narrow > 1:
        right = lax.all_gather(right, "narrow", axis=3, tiled=True)
    tri = jnp.einsum("sckj,scki->cji", right, left, preferred_element_type=jnp.float32)
    back = tri.astype(jnp.bfloat16).reshape(per_device, wide, tile_cols, tile_rows)
    back = jnp.transpose(back, (1, 0, 2, 3))
    tri = lax.all_to_all(back, "wide", split_axis=0, concat_axis=0, tiled=True)
    tri = tri.reshape(C, tile_cols, tile_rows).astype(jnp.float32)
    centre = jnp.mean(tri, axis=0, keepdims=True)
    spread = jnp.mean(jnp.square(tri - centre), axis=0, keepdims=True)
    tri_normed = ((tri - centre) * lax.rsqrt(spread + 1e-05)).astype(jnp.bfloat16)
    gate = jax.nn.sigmoid(
        jnp.einsum("ikc,cd->ikd", normed, gate_weight, preferred_element_type=jnp.float32)
    )
    return gate * jnp.einsum(
        "cji,cd->ijd", tri_normed, out_weight, preferred_element_type=jnp.float32
    )


def solution(mesh):
    return jax.shard_map(
        on_device,
        mesh=mesh,
        in_specs=(P("narrow", "wide", None), P(), P(), P(), P(), P()),
        out_specs=P("narrow", "wide", None),
        check_vma=False,
    )
```

time: 179 us -> 65.3 us (0.36)
  waiting for transfers between devices: 136 us -> 0 us
  blocking collectives: 0 us -> 52.3 us
  between operations: 13.6 us -> 0.18 us
  starting transfers between devices: 7.3 us -> 0 us
  matrix products: 10.9 us -> 4.52 us
  local copies, waits for them, and re-layouts: 5.1 us -> 2.33 us
    all_gather x1 -> x0, waiting for transfers between devices: 116 us -> none  [on_device(): lax.all_gather(left_proj, 'wide', axis=1, tiled=True)]
    all_to_all x0 -> x2, blocking collectives: none -> 52.3 us  [the longest x1 33.4 us: on_device(): recv = lax.all_to_all(send, 'wide', split_axis=0, concat_axis=0, tiled=True)]
    all_to_all x1 -> x0, waiting for transfers between devices: 20.2 us -> none  [on_device(): lax.all_to_all(right_all, 'wide', split_axis=0, concat_axis=1, tiled=True)]
    all_to_all x1 -> x0, starting transfers between devices: 7.3 us -> none  [on_device(): lax.all_to_all(right_all, 'wide', split_axis=0, concat_axis=1, tiled=True)]
    dot_general x6, matrix products: 10.9 us -> 4.52 us  [the longest x2 2.3 us: edges(): jnp.einsum('cd,ikc->dki', weight, normed, preferred_element_type=jnp.floa...]
    reshape x2 -> x1, local copies, waits for them, and re-layouts: 2.3 us -> 0.05 us  [on_device(): tri.astype(jnp.bfloat16).reshape(per_device, wide, tile_cols, tile_rows)]
    reshape x3 -> x0, other arithmetic: 2.14 us -> none  [the longest x1 1.25 us: on_device(): gated_projection(normed, left_weight, C).reshape(tile_rows, tile_cols, C)]
    convert_element_type x2 -> x0, local copies, waits for them, and re-layouts: 1.89 us -> none  [the longest x1 1.32 us: on_device(): right_proj = (gated_projection(normed, right_weight, C).reshape(tile_rows...]
  transfers between devices with their start and end apart: 2 -> 0, of which waited for: 2 -> 0; matrix products, arithmetic and copies ran while one was open for 1% -> 0% of each run, Pallas kernels for 0% -> 0%
where the time goes in v1:
time: 65.3 us; the launch traced here: 65 us
  blocking collectives  52.3 us (80%)
  other arithmetic  5.67 us (9%)
  matrix products  4.52 us (7%)
  local copies, waits for them, and re-layouts  2.33 us (4%)
    all_to_all x1, blocking collectives, on_device(): recv = lax.all_to_all(send, 'wide', split_axis=0, concat_axis=0, tiled=True)  33.4 us
    all_to_all x1, blocking collectives, on_device(): tri = lax.all_to_all(back, 'wide', split_axis=0, concat_axis=0, tiled=True)  19 us
    dot_general x2, matrix products, edges(): jnp.einsum('cd,ikc->dki', weight, normed, preferred_element_type=jnp.floa...  2.3 us
    convert_element_type x1, other arithmetic, edges(): proj.astype(jnp.bfloat16).reshape(wide, per_device, tile_cols, tile_rows)  2.13 us
    reduce_sum x1, other arithmetic, on_device(): centre = jnp.mean(pair_act, axis=-1, keepdims=True)  1.66 us
    mul x1, local copies, waits for them, and re-layouts, on_device(): gate * jnp.einsum('cji,cd->ijd', tri_normed, out_weight, preferred_elemen...  1.58 us

profile of v1, /device:TPU:0, one launch (start us, length us, event | category | flops | bytes accessed | tf_op | source)
XLA Modules:
  0.0 65.0 jit_solution(17848403901525676128)
XLA Ops:
  0.0 1.7 %reduce_sum.36 = f32[256,8]{1,0:T(8,128)S(1)} reduce(f32[256,8,128]{2,1,0:T(8,128)} %param.6, f32[]{:T(128)} %constant.42.clone.1), dimensions={2}, to_apply=%region_0.1 | reduce | flops 260096 | bytes 1056772 | tf_op jit(solution)/shard_map/reduce_sum | solution.py:23
  1.7 0.6 multiply_reduce_fusion.1
  2.4 0.0 copy-start.2
  2.4 0.6 multiply_convert_fusion
  3.0 0.0 copy-start.5
  3.0 0.5 convolution_bitcast_fusion.1
  3.5 1.8 %convolution_bitcast_fusion = f32[256,8,256]{2,0,1:T(8,128)} fusion(bf16[256,8,128]{2,1,0:T(8,128)(2,1)S(1)} %multiply_convert_fusion, bf16[128,256]{1,0:T(8,128)(2,1)S(1)} %copy-done.2), kind=kOutput, calls=%fused_computation | convolution fusion | flops 134217728 | bytes 2686976 | tf_op jit(solution)/shard_map/cd,ikc->dki/dot_general | solution.py:28
  5.4 0.3 fusion.6
  5.7 2.1 %fusion.15 = (bf16[128,8,256]{2,0,1:T(8,128)(2,1)S(1)}, bf16[128,8,256]{2,0,1:T(8,128)(2,1)S(1)}) fusion(f32[256,8,256]{2,0,1:T(8,128)S(1)} %convolution_bitcast_fusion.1, f32[8,256]{1,0:T(8,128)S(1)} %fusion.6, f32[256,8,256]{2,0,1:T(8,128)} %convolution_bitcast_fusion), kind=kLoop, calls=%fused_computation.22 | loop fusion | flops 3145728 | bytes 5251072 | tf_op jit(solution)/shard_map/convert_element_type | solution.py:30
  7.8 0.3 copy.42
  8.1 0.3 copy.44
  8.4 0.1 pad_maximum_fusion
  8.5 33.4 %all_to_all.10 = bf16[32,2,4,8,256]{4,3,2,1,0:T(8,128)(2,1)S(1)} all-to-all(bf16[32,2,4,8,256]{4,3,2,1,0:T(8,128)(2,1)S(1)} %pad_maximum_fusion), channel_id=1, replica_groups=mesh['narrow'=1,'wide'=32] {'wide'}, dimensions={0} | all-to-all | bytes 2097152 | tf_op jit(solution)/shard_map/all_to_all | solution.py:33
  41.9 0.1 fusion.34
  42.0 1.1 %fusion.5 = bf16[4,32,8,256]{3,2,1,0:T(8,128)(2,1)S(1)} fusion(bf16[32,1,4,8,256]{4,3,2,1,0:T(8,128)(2,1)S(1)} %get-tuple-element.6, bf16[32,1,4,8,256]{4,3,2,1,0:T(8,128)(2,1)S(1)} %get-tuple-element.5), kind=kOutput, calls=%fused_computation.10 | convolution fusion | flops 134479872 | bytes 1572864 | tf_op jit(solution)/shard_map/sckj,scki->cji/dot_general | solution.py:37
  43.1 0.0 copy-start.3
  43.1 0.1 copy.60
  43.2 19.0 %all_to_all.11 = bf16[32,4,8,256]{3,2,1,0:T(8,128)(2,1)S(1)} all-to-all(bf16[32,4,8,256]{3,2,1,0:T(8,128)(2,1)S(1)} %bitcast.44), channel_id=1, replica_groups=mesh['narrow'=1,'wide'=32] {'wide'}, dimensions={0} | all-to-all | bytes 1048576 | tf_op jit(solution)/shard_map/all_to_all | solution.py:40
  62.1 0.1 convert_reduce_fusion
  62.3 0.2 multiply_reduce_fusion
  62.5 0.1 fusion.20
  62.6 0.3 convolution_bitcast_fusion.2
  63.0 0.4 fusion.3
  63.4 1.6 %copy.37 = f32[256,8,128]{2,1,0:T(8,128)} copy(f32[256,8,128]{2,0,1:T(8,128)S(1)} %fusion.3) | data formatting | bytes 2097152 | tf_op jit(solution)/shard_map/mul | solution.py:48
  (15 shorter events, 0.1 us)
Async XLA Ops:
  0.0 3.0 %copy-start = (bf16[128,256]{1,0:T(8,128)(2,1)S(1)}, bf16[128,256]{1,0:T(8,128)(2,1)}, u32[]{:S(2)}) copy-start(bf16[128,256]{1,0:T(8,128)(2,1)} %param.8) | copy-start | bytes 196612
  0.0 1.7 %copy-start.1 = (f32[256,8,128]{2,1,0:T(8,128)S(1)}, f32[256,8,128]{2,1,0:T(8,128)}, u32[]{:S(2)}) copy-start(f32[256,8,128]{2,1,0:T(8,128)} %param.6) | copy-start | bytes 3145732
  2.4 1.1 %copy-start.2 = (bf16[128,256]{1,0:T(8,128)(2,1)S(1)}, bf16[128,256]{1,0:T(8,128)(2,1)}, u32[]{:S(2)}) copy-start(bf16[128,256]{1,0:T(8,128)(2,1)} %param.9) | copy-start | bytes 196612
  3.0 2.3 %copy-start.5 = (s32[4,4]{1,0:T(4,128)S(1)}, s32[4,4]{1,0:T(4,128)}, u32[]{:S(2)}) copy-start(s32[4,4]{1,0:T(4,128)} %param.7) | copy-start | bytes 196
  43.1 19.6 %copy-start.3 = (bf16[128,128]{1,0:T(8,128)(2,1)S(1)}, bf16[128,128]{1,0:T(8,128)(2,1)}, u32[]{:S(2)}) copy-start(bf16[128,128]{1,0:T(8,128)(2,1)} %param.11) | copy-start | bytes 98308
  62.1 0.9 %copy-start.4 = (bf16[128,128]{1,0:T(8,128)(2,1)S(1)}, bf16[128,128]{1,0:T(8,128)(2,1)}, u32[]{:S(2)}) copy-start(bf16[128,128]{1,0:T(8,128)(2,1)} %param.10) | copy-start | bytes 98308
